TPU v7x, 256 devices: a whole 4x4x8 slice. The times are simulated.
256 devices in a mesh: loop: 128 (over y_hi, x, z, core), sub: 2 (over y_lo).
Axes of the slice: x: 4, y: 4 (y_hi: 2, y_lo: 2; y = y_hi * 2 + y_lo), z: 8, core: 2. Of those that a mesh axis runs over, the one named last changes fastest.
Arguments:
- embeddings: bfloat16 [65536, 1024], P(('loop', 'sub')), may hold values from -10 to 10
- reward: float32 [65536], P(('loop', 'sub')), may hold values from 0.5 to 13.5
- partner: int32 [65536], P(('loop', 'sub')), may hold values from 0 to 65535, as said below
- policy: int32 [65536], P(('loop', 'sub')), may hold values from 0 to 15
Outputs:
- weighted_loss: float32 [65536], P(('loop', 'sub'))
- gradient: float32 [65536, 1024], P(('loop', 'sub'))
- policy_loss: float32 [16], replicated
Inputs may be any that keep to these rules, and one draw needn't show every extreme that they name: partner_i is a view other than i in the same block of 512 views, and partner of partner_i is i.
All inputs are finite; a program needn't handle non-finite values.
Results may differ from a plain program's by a relative error of at most 0.0029.
Values may be sent and summed in bfloat16 or wider, within the bound.
A program may use at most 64 MiB of HBM per device.

v0:
```python
from functools import reduce
import math

import jax
import jax.numpy as jnp
from jax import lax
from jax.sharding import PartitionSpec as P

RADIUS = 4
POLICIES = 16


def passed_along(value, axis, steps):
    count = lax.axis_size(axis)
    pairs = [(source, (source + steps) % count) for source in range(count)]
    return lax.ppermute(value, axis, pairs)


def key_scores(queries, key_block, factor):
    return (
        lax.dot_general(
            queries, key_block, (((1,), (1,)), ((), ())), preferred_element_type=jnp.float32
        )
        * factor
    )


def arrivals(payload):
    lower_list = []
    upper_list = []
    for distance in range(1, RADIUS + 1):
        lower_list.append(passed_along(payload, "loop", distance))
        upper_list.append(passed_along(payload, "loop", -distance))
    return lower_list + upper_list


def body(embeddings, reward, partner, policy):
    row_count, feature_width = embeddings.shape
    loop_count = lax.axis_size("loop")
    sub_count = lax.axis_size("sub")
    block_size = row_count * sub_count
    loop_at = lax.axis_index("loop")
    sub_at = lax.axis_index("sub")
    factor = 1.0 / math.sqrt(feature_width)
    local_block = lax.all_gather(embeddings, "sub", axis=0, tiled=True)
    remote = arrivals(local_block)
    key_blocks = [local_block] + remote
    score_tiles = [key_scores(embeddings, key_block, factor) for key_block in key_blocks]
    columns = lax.broadcasted_iota(jnp.int32, (row_count, block_size), 1)
    own_rows = lax.broadcasted_iota(jnp.int32, (row_count, block_size), 0) + sub_at * row_count
    score_tiles[0] = jnp.where(columns == own_rows, -jnp.inf, score_tiles[0])
    matched = columns == (partner - loop_at * block_size)[:, None]
    positive = jnp.sum(jnp.where(matched, score_tiles[0], 0.0), axis=1)
    row_max = reduce(jnp.maximum, [jnp.max(score_tile, axis=1) for score_tile in score_tiles])
    row_total = reduce(
        jnp.add,
        [jnp.sum(jnp.exp(score_tile - row_max[:, None]), axis=1) for score_tile in score_tiles],
    )
    log_total = row_max + jnp.log(row_total)
    weighted = reward * (log_total - positive)
    labels = policy[:, None] == jnp.arange(POLICIES, dtype=jnp.int32)[None, :]
    partial_sum = jnp.sum(jnp.where(labels, weighted[:, None], 0.0), axis=0)
    policy_loss = lax.psum(partial_sum, ("loop", "sub")) * (POLICIES / (block_size * loop_count))
    own_stats = jnp.stack([log_total, reward])
    local_stats = lax.all_gather(own_stats, "sub", axis=1, tiled=True)
    lower_stats = []
    upper_stats = []
    for distance in range(1, RADIUS + 1):
        lower_stats.append(passed_along(local_stats, "loop", distance))
        upper_stats.append(passed_along(local_stats, "loop", -distance))
    remote_stats = lower_stats + upper_stats
    stats_list = [local_stats] + remote_stats
    partner_weight = jnp.sum(jnp.where(matched, local_stats[1][None, :], 0.0), axis=1)
    gradient = jnp.zeros((row_count, feature_width), jnp.float32)
    for number in range(len(key_blocks)):
        score_tile = score_tiles[number]
        block_stats = stats_list[number]
        coefficient = reward[:, None] * jnp.exp(score_tile - log_total[:, None]) + block_stats[1][
            None, :
        ] * jnp.exp(score_tile - block_stats[0][None, :])
        if number == 0:
            coefficient = coefficient - jnp.where(matched, (reward + partner_weight)[:, None], 0.0)
        gradient = gradient + jnp.dot(
            coefficient.astype(jnp.bfloat16), key_blocks[number], preferred_element_type=jnp.float32
        )
    return (weighted, gradient, policy_loss)


def solution(mesh):
    in_specs = (
        P(("loop", "sub"), None),
        P(("loop", "sub")),
        P(("loop", "sub")),
        P(("loop", "sub")),
    )
    out_specs = (P(("loop", "sub")), P(("loop", "sub"), None), P())
    return jax.shard_map(body, mesh=mesh, in_specs=in_specs, out_specs=out_specs, check_vma=False)
```

profile of v0, /device:TPU:1, one launch (start us, length us, event | category | flops | bytes accessed | tf_op | source)
XLA Modules:
  0.0 289.4 jit_solution(7246175838195063988)
XLA Ops:
  7.2 0.7 all-gather.2.cloned.1.call-update
  7.9 32.1 %all-gather.2.cloned.1.call-done = bf16[512,1024]{1,0:T(8,128)(2,1)} async-done(((bf16[256,1024]{1,0:T(8,128)(2,1)}), bf16[512,1024]{1,0:T(8,128)(2,1)}) %all-gather.2.cloned.1.call-update) | async-done | bytes 1048592 | tf_op jit(solution)/shard_map/all_gather | solution.py:45
  40.0 8.1 %collective-permute-start.7 = (bf16[512,1024]{1,0:T(8,128)(2,1)}, bf16[512,1024]{1,0:T(8,128)(2,1)S(1)}, u32[]{:S(2)}, u32[]{:S(2)}) collective-permute-start(bf16[512,1024]{1,0:T(8,128)(2,1)} %all-gather.2.cloned.1.call-done), channel_id=1, source_target_pairs={{0,248},{2,250},{4,252},{6,254},{8,0},{10,2},{12,4},{14,6},{16,8},... | collective-permute-start | bytes 3145736 | tf_op jit(solution)/shard_map/ppermute | solution.py:16
  48.2 1.9 collective-permute-start.6
  50.1 1.1 collective-permute-start.5
  51.2 1.1 collective-permute-start.3
  52.3 1.8 fusion.70
  54.1 38.7 %collective-permute-done.7 = bf16[512,1024]{1,0:T(8,128)(2,1)S(1)} collective-permute-done((bf16[512,1024]{1,0:T(8,128)(2,1)}, bf16[512,1024]{1,0:T(8,128)(2,1)S(1)}, u32[]{:S(2)}, u32[]{:S(2)}) %collective-permute-start.7) | collective-permute-done | bytes 1048608 | tf_op jit(solution)/shard_map/ppermute | solution.py:16
  92.9 1.1 collective-permute-start.2
  94.5 32.8 %collective-permute-done.6 = bf16[512,1024]{1,0:T(8,128)(2,1)S(1)} collective-permute-done((bf16[512,1024]{1,0:T(8,128)(2,1)}, bf16[512,1024]{1,0:T(8,128)(2,1)S(1)}, u32[]{:S(2)}, u32[]{:S(2)}) %collective-permute-start.6) | collective-permute-done | bytes 1048608 | tf_op jit(solution)/shard_map/ppermute | solution.py:16
  128.3 21.6 %collective-permute-done.5 = bf16[512,1024]{1,0:T(8,128)(2,1)S(1)} collective-permute-done((bf16[512,1024]{1,0:T(8,128)(2,1)}, bf16[512,1024]{1,0:T(8,128)(2,1)S(1)}, u32[]{:S(2)}, u32[]{:S(2)}) %collective-permute-start.5) | collective-permute-done | bytes 1048608 | tf_op jit(solution)/shard_map/ppermute | solution.py:16
  150.9 9.2 %collective-permute-done.4 = bf16[512,1024]{1,0:T(8,128)(2,1)S(1)} collective-permute-done((bf16[512,1024]{1,0:T(8,128)(2,1)}, bf16[512,1024]{1,0:T(8,128)(2,1)S(1)}, u32[]{:S(2)}, u32[]{:S(2)}) %collective-permute-start.4) | collective-permute-done | bytes 1048608 | tf_op jit(solution)/shard_map/ppermute | solution.py:16
  165.3 0.9 select_reduce_fusion.1
  166.2 0.7 copy-done.24
  166.9 3.7 %all_gather.7 = f32[2,512]{1,0:T(2,128)S(1)} all-gather(f32[2,256]{1,0:T(2,128)S(1)} %pad_maximum_fusion), channel_id=1, replica_groups=mesh['loop'=128,'sub'=2] {'sub'}, dimensions={1}, use_global_device_ids=true | all-gather | bytes 6144 | tf_op jit(solution)/shard_map/all_gather | solution.py:65
  170.6 6.9 %collective-permute-start.15 = (f32[2,512]{1,0:T(2,128)S(1)}, f32[2,512]{1,0:T(2,128)S(1)}, u32[]{:S(2)}, u32[]{:S(2)}) collective-permute-start(f32[2,512]{1,0:T(2,128)S(1)} %all_gather.7), channel_id=1, source_target_pairs={{0,248},{2,250},{4,252},{6,254},{8,0},{10,2},{12,4},{14,6},{16,8},... | collective-permute-start | bytes 12296 | tf_op jit(solution)/shard_map/ppermute | solution.py:16
  177.6 2.7 collective-permute-start.14
  180.8 2.4 collective-permute-start.11
  183.4 0.7 copy-done.27
  184.1 75.9 %psum.7 = f32[16]{0:T(128)S(1)} all-reduce(f32[16]{0:T(128)S(1)} %select_reduce_fusion.2), channel_id=1, replica_groups=mesh['loop'=128,'sub'=2] {'loop','sub'}, use_global_device_ids=true, to_apply=%region_21.22 | all-reduce | flops 16 | bytes 128 | tf_op jit(solution)/shard_map/psum | solution.py:63
  260.1 2.1 fusion.7
  263.3 0.9 collective-permute-start.9
  264.2 7.2 %collective-permute-done.10 = f32[2,512]{1,0:T(2,128)S(1)} collective-permute-done((f32[2,512]{1,0:T(2,128)S(1)}, f32[2,512]{1,0:T(2,128)S(1)}, u32[]{:S(2)}, u32[]{:S(2)}) %collective-permute-start.10) | collective-permute-done | bytes 4128 | tf_op jit(solution)/shard_map/ppermute | solution.py:16
  280.9 1.7 fusion.5
  (108 shorter events, 19.2 us)
Async XLA Ops:
  7.2 45.1 %copy-start = (bf16[256,1024]{1,0:T(8,128)(2,1)S(1)}, bf16[256,1024]{1,0:T(8,128)(2,1)}, u32[]{:S(2)}) copy-start(bf16[256,1024]{1,0:T(8,128)(2,1)} %param.4) | copy-start | bytes 1572868
  7.2 32.9 %all-gather.2.cloned.1.call-start = ((), (), s32[]{:S(2)}) async-start(), calls=%async_computation | async-start | bytes 1572864 | tf_op jit(solution)/shard_map/all_gather | solution.py:45
  40.0 52.8 %collective-permute-start.7 = (bf16[512,1024]{1,0:T(8,128)(2,1)}, bf16[512,1024]{1,0:T(8,128)(2,1)S(1)}, u32[]{:S(2)}, u32[]{:S(2)}) collective-permute-start(bf16[512,1024]{1,0:T(8,128)(2,1)} %all-gather.2.cloned.1.call-done), channel_id=1, source_target_pairs={{0,248},{2,250},{4,252},{6,254},{8,0},{10,2},{12,4},{14,6},{16,8},... | collective-permute-start | bytes 3145736 | tf_op jit(solution)/shard_map/ppermute | solution.py:16
  48.2 79.1 %collective-permute-start.6 = (bf16[512,1024]{1,0:T(8,128)(2,1)}, bf16[512,1024]{1,0:T(8,128)(2,1)S(1)}, u32[]{:S(2)}, u32[]{:S(2)}) collective-permute-start(bf16[512,1024]{1,0:T(8,128)(2,1)} %all-gather.2.cloned.1.call-done), channel_id=1, source_target_pairs={{0,250},{2,252},{4,254},{6,0},{8,2},{10,4},{12,6},{14,8},{16,10},{... | collective-permute-start | bytes 3145736 | tf_op jit(solution)/shard_map/ppermute | solution.py:16
  50.1 99.8 %collective-permute-start.5 = (bf16[512,1024]{1,0:T(8,128)(2,1)}, bf16[512,1024]{1,0:T(8,128)(2,1)S(1)}, u32[]{:S(2)}, u32[]{:S(2)}) collective-permute-start(bf16[512,1024]{1,0:T(8,128)(2,1)} %all-gather.2.cloned.1.call-done), channel_id=1, source_target_pairs={{0,252},{2,254},{4,0},{6,2},{8,4},{10,6},{12,8},{14,10},{16,12},{1... | collective-permute-start | bytes 3145736 | tf_op jit(solution)/shard_map/ppermute | solution.py:16
  51.2 41.7 %copy-start.28 = (bf16[512,1024]{1,0:T(8,128)(2,1)S(1)}, bf16[512,1024]{1,0:T(8,128)(2,1)}, u32[]{:S(2)}) copy-start(bf16[512,1024]{1,0:T(8,128)(2,1)} %all-gather.2.cloned.1.call-done) | copy-start | bytes 3145732
  51.2 108.9 %collective-permute-start.4 = (bf16[512,1024]{1,0:T(8,128)(2,1)}, bf16[512,1024]{1,0:T(8,128)(2,1)S(1)}, u32[]{:S(2)}, u32[]{:S(2)}) collective-permute-start(bf16[512,1024]{1,0:T(8,128)(2,1)} %all-gather.2.cloned.1.call-done), channel_id=1, source_target_pairs={{0,254},{2,0},{4,2},{6,4},{8,6},{10,8},{12,10},{14,12},{16,14},{18... | collective-permute-start | bytes 3145736 | tf_op jit(solution)/shard_map/ppermute | solution.py:16
  51.2 109.9 %collective-permute-start.3 = (bf16[512,1024]{1,0:T(8,128)(2,1)}, bf16[512,1024]{1,0:T(8,128)(2,1)S(1)}, u32[]{:S(2)}, u32[]{:S(2)}) collective-permute-start(bf16[512,1024]{1,0:T(8,128)(2,1)} %all-gather.2.cloned.1.call-done), channel_id=1, source_target_pairs={{0,8},{2,10},{4,12},{6,14},{8,16},{10,18},{12,20},{14,22},{16,24},... | collective-permute-start | bytes 3145736 | tf_op jit(solution)/shard_map/ppermute | solution.py:16
  54.1 111.2 %copy-start.23 = (f32[256,512]{1,0:T(8,128)}, f32[256,512]{1,0:T(8,128)S(1)}, u32[]{:S(2)}) copy-start(f32[256,512]{1,0:T(8,128)S(1)} %get-tuple-element.48) | copy-start | bytes 1572868
  92.9 34.4 %copy-start.11 = (bf16[512,1024]{1,0:T(8,128)(2,1)}, bf16[512,1024]{1,0:T(8,128)(2,1)S(1)}, u32[]{:S(2)}) copy-start(bf16[512,1024]{1,0:T(8,128)(2,1)S(1)} %collective-permute-done.7) | copy-start | bytes 3145732
  92.9 69.3 %collective-permute-start.2 = (bf16[512,1024]{1,0:T(8,128)(2,1)S(1)}, bf16[512,1024]{1,0:T(8,128)(2,1)S(1)}, u32[]{:S(2)}, u32[]{:S(2)}) collective-permute-start(bf16[512,1024]{1,0:T(8,128)(2,1)S(1)} %copy-done.28), channel_id=1, source_target_pairs={{0,6},{2,8},{4,10},{6,12},{8,14},{10,16},{12,18},{14,20},{16,22},{... | collective-permute-start | bytes 3145736 | tf_op jit(solution)/shard_map/ppermute | solution.py:16
  127.3 35.9 %collective-permute-start.1 = (bf16[512,1024]{1,0:T(8,128)(2,1)S(1)}, bf16[512,1024]{1,0:T(8,128)(2,1)S(1)}, u32[]{:S(2)}, u32[]{:S(2)}) collective-permute-start(bf16[512,1024]{1,0:T(8,128)(2,1)S(1)} %copy-done.28), channel_id=1, source_target_pairs={{0,4},{2,6},{4,8},{6,10},{8,12},{10,14},{12,16},{14,18},{16,20},{1... | collective-permute-start | bytes 3145736 | tf_op jit(solution)/shard_map/ppermute | solution.py:16
  149.9 14.4 %collective-permute-start = (bf16[512,1024]{1,0:T(8,128)(2,1)S(1)}, bf16[512,1024]{1,0:T(8,128)(2,1)S(1)}, u32[]{:S(2)}, u32[]{:S(2)}) collective-permute-start(bf16[512,1024]{1,0:T(8,128)(2,1)S(1)} %copy-done.28), channel_id=1, source_target_pairs={{0,2},{2,4},{4,6},{6,8},{8,10},{10,12},{12,14},{14,16},{16,18},{18... | collective-permute-start | bytes 3145736 | tf_op jit(solution)/shard_map/ppermute | solution.py:16
  162.2 3.1 %copy-start.1 = (f32[256,512]{1,0:T(8,128)}, f32[256,512]{1,0:T(8,128)S(1)}, u32[]{:S(2)}) copy-start(f32[256,512]{1,0:T(8,128)S(1)} %get-tuple-element.42) | copy-start | bytes 1572868
  166.9 16.5 %copy-start.25 = (f32[256]{0:T(256)}, f32[256]{0:T(256)S(1)}, u32[]{:S(2)}) copy-start(f32[256]{0:T(256)S(1)} %get-tuple-element.13) | copy-start | bytes 3076
  170.6 92.0 %collective-permute-start.15 = (f32[2,512]{1,0:T(2,128)S(1)}, f32[2,512]{1,0:T(2,128)S(1)}, u32[]{:S(2)}, u32[]{:S(2)}) collective-permute-start(f32[2,512]{1,0:T(2,128)S(1)} %all_gather.7), channel_id=1, source_target_pairs={{0,248},{2,250},{4,252},{6,254},{8,0},{10,2},{12,4},{14,6},{16,8},... | collective-permute-start | bytes 12296 | tf_op jit(solution)/shard_map/ppermute | solution.py:16
  177.6 85.6 %collective-permute-start.14 = (f32[2,512]{1,0:T(2,128)S(1)}, f32[2,512]{1,0:T(2,128)S(1)}, u32[]{:S(2)}, u32[]{:S(2)}) collective-permute-start(f32[2,512]{1,0:T(2,128)S(1)} %all_gather.7), channel_id=1, source_target_pairs={{0,250},{2,252},{4,254},{6,0},{8,2},{10,4},{12,6},{14,8},{16,10},{... | collective-permute-start | bytes 12296 | tf_op jit(solution)/shard_map/ppermute | solution.py:16
  180.2 83.1 %collective-permute-start.13 = (f32[2,512]{1,0:T(2,128)S(1)}, f32[2,512]{1,0:T(2,128)S(1)}, u32[]{:S(2)}, u32[]{:S(2)}) collective-permute-start(f32[2,512]{1,0:T(2,128)S(1)} %all_gather.7), channel_id=1, source_target_pairs={{0,252},{2,254},{4,0},{6,2},{8,4},{10,6},{12,8},{14,10},{16,12},{1... | collective-permute-start | bytes 12296 | tf_op jit(solution)/shard_map/ppermute | solution.py:16
  180.4 83.8 %collective-permute-start.12 = (f32[2,512]{1,0:T(2,128)S(1)}, f32[2,512]{1,0:T(2,128)S(1)}, u32[]{:S(2)}, u32[]{:S(2)}) collective-permute-start(f32[2,512]{1,0:T(2,128)S(1)} %all_gather.7), channel_id=1, source_target_pairs={{0,254},{2,0},{4,2},{6,4},{8,6},{10,8},{12,10},{14,12},{16,14},{18... | collective-permute-start | bytes 12296 | tf_op jit(solution)/shard_map/ppermute | solution.py:16
  180.8 83.4 %collective-permute-start.11 = (f32[2,512]{1,0:T(2,128)S(1)}, f32[2,512]{1,0:T(2,128)S(1)}, u32[]{:S(2)}, u32[]{:S(2)}) collective-permute-start(f32[2,512]{1,0:T(2,128)S(1)} %all_gather.7), channel_id=1, source_target_pairs={{0,8},{2,10},{4,12},{6,14},{8,16},{10,18},{12,20},{14,22},{16,24},... | collective-permute-start | bytes 12296 | tf_op jit(solution)/shard_map/ppermute | solution.py:16
  260.1 11.7 %copy-start.12 = (bf16[512,1024]{1,0:T(8,128)(2,1)S(1)}, bf16[512,1024]{1,0:T(8,128)(2,1)}, u32[]{:S(2)}) copy-start(bf16[512,1024]{1,0:T(8,128)(2,1)} %copy-done.11) | copy-start | bytes 3145732
  262.7 8.8 %collective-permute-start.10 = (f32[2,512]{1,0:T(2,128)S(1)}, f32[2,512]{1,0:T(2,128)S(1)}, u32[]{:S(2)}, u32[]{:S(2)}) collective-permute-start(f32[2,512]{1,0:T(2,128)S(1)} %all_gather.7), channel_id=1, source_target_pairs={{0,6},{2,8},{4,10},{6,12},{8,14},{10,16},{12,18},{14,20},{16,22},{... | collective-permute-start | bytes 12296 | tf_op jit(solution)/shard_map/ppermute | solution.py:16
  263.2 8.2 %collective-permute-start.8 = (f32[2,512]{1,0:T(2,128)S(1)}, f32[2,512]{1,0:T(2,128)S(1)}, u32[]{:S(2)}, u32[]{:S(2)}) collective-permute-start(f32[2,512]{1,0:T(2,128)S(1)} %all_gather.7), channel_id=1, source_target_pairs={{0,2},{2,4},{4,6},{6,8},{8,10},{10,12},{12,14},{14,16},{16,18},{18... | collective-permute-start | bytes 12296 | tf_op jit(solution)/shard_map/ppermute | solution.py:16
  263.3 8.5 %collective-permute-start.9 = (f32[2,512]{1,0:T(2,128)S(1)}, f32[2,512]{1,0:T(2,128)S(1)}, u32[]{:S(2)}, u32[]{:S(2)}) collective-permute-start(f32[2,512]{1,0:T(2,128)S(1)} %all_gather.7), channel_id=1, source_target_pairs={{0,4},{2,6},{4,8},{6,10},{8,12},{10,14},{12,16},{14,18},{16,20},{1... | collective-permute-start | bytes 12296 | tf_op jit(solution)/shard_map/ppermute | solution.py:16
  (22 other events, 24.7 us)
Sparse Core Ops, SparseCore 0:
  9.8 30.1 all-gather.1
where the time goes:
time: 290 us; the launch traced here: 289 us
  waiting for transfers between devices  143 us (49%)
  blocking collectives  79.7 us (27%)
  starting transfers between devices  27.3 us (9%)
  between operations  14.3 us (5%)
  matrix products  14.1 us (5%)
  local copies, waits for them, and re-layouts  9.46 us (3%)
    ppermute x16, waiting for transfers between devices, passed_along(): return lax.ppermute(value, axis, pairs)  110 us
    psum x1, blocking collectives, body(): lax.psum(partial_sum, ('loop', 'sub'))  75.9 us
    all_gather x1, waiting for transfers between devices, body(): local_block = lax.all_gather(embeddings, 'sub', axis=0, tiled=True)  32.1 us
    ppermute x16, starting transfers between devices, passed_along(): return lax.ppermute(value, axis, pairs)  27.3 us
    unnamed x58, local copies, waits for them, and re-layouts  9.41 us
    dot_general x9, matrix products, body(): jnp.dot(coefficient.astype(jnp.bfloat16), key_blocks[number], preferred_e...  7.8 us
    dot_general x9, matrix products, key_scores(): lax.dot_general(queries, key_block, (((1,), (1,)), ((), ())), preferred_e...  6.27 us
  transfers between devices with their start and end apart: 17, of which 8 were waited for; matrix products, arithmetic and copies ran while one was open for 3% of the time, Pallas kernels for 0%

commit v1 on v0

v1 whole, which is shorter than its diff:
```python
import functools
import math

import jax
import jax.numpy as jnp
from jax import lax
from jax.experimental import pallas as pl
from jax.experimental.pallas import tpu as pltpu
from jax.sharding import PartitionSpec as P

RADIUS = 4
POLICIES = 16
ROWS = 256
WIDTH = 1024
SUBS = 2
BLOCK = ROWS * SUBS
LOOP = 128
SEAM = 64
CHUNKS = 4
TILE = 256
PART = ROWS // CHUNKS
SLOTS = (2 * RADIUS + 1) * SUBS
GROUP = 16
LOG2E = 1.4426950408889634
LN2 = 0.6931471805599453
LOWEST = -1e30
MESH = pl.DeviceIdType.MESH

LOW_OWN, LOW_HALF, LOW_FAR, UP_OWN, UP_HALF, UP_FAR, SUB_OWN, SUB_LOW, SUB_UP = range(9)
CORE_OWN, CORE_HALF, CORE_LOW_A, CORE_LOW_B, CORE_UP_A, CORE_UP_B, CORE_FAR_A, CORE_FAR_B = range(9, 17)
CLASSES = 17


def slot(offset, half):
    return (offset + RADIUS) * SUBS + half


def kernel(
    x_ref, reward_ref, partner_ref, policy_ref,
    weighted_ref, gradient_ref, loss_ref,
    keys, scores, weights, level, rewards, first_sum, second_sum,
    recv, send, level_sem, sum_sem, reward_sem, local_sem,
):
    block = lax.axis_index("loop")
    sub = lax.axis_index("sub")
    core = lax.rem(block, 2)

    def crosses(at):
        return jnp.where(lax.rem(at, SEAM) >= SEAM - 2, 1, 0)

    def flip(half, by):
        return half + by - 2 * half * by

    def at_loop(index):
        return lax.rem(index + LOOP, LOOP)

    cross_up = crosses(block)
    cross_low = crosses(at_loop(block - 2))
    cross_up2 = crosses(at_loop(block + 2))
    cross_low2 = crosses(at_loop(block - 4))
    up_dev = (at_loop(block + 2), flip(sub, cross_up))
    low_dev = (at_loop(block - 2), flip(sub, cross_low))
    sub_dev = (block, 1 - sub)
    core_dev = (block + 1 - 2 * core, sub)
    low_half = flip(sub, cross_low)
    up_half = flip(sub, cross_up)
    low_far = flip(low_half, cross_low2)
    up_far = flip(up_half, cross_up2)

    own_slot = slot(0, sub)
    half_slot = slot(0, 1 - sub)

    def piece(index):
        return pl.ds(pl.multiple_of(index * ROWS, ROWS), ROWS)

    load = pltpu.make_async_copy(x_ref, keys.at[piece(own_slot)], local_sem)
    load.start()

    targets = [up_dev, low_dev, sub_dev, core_dev]
    level_targets = []
    for offset in range(-RADIUS, RADIUS + 1):
        for other in range(SUBS):
            if offset == 0 and other == 0:
                continue
            level_targets.append((offset, (at_loop(block + offset), flip(sub, other))))
    line = lax.rem(block, GROUP)
    line_base = block - line
    first_targets = [(line_base + lax.rem(line + i, GROUP), sub) for i in range(1, GROUP)]
    plane = (block // GROUP) * SUBS + sub
    second_targets = []
    for i in range(1, GROUP):
        other = lax.rem(plane + i, GROUP)
        second_targets.append(((other // SUBS) * GROUP + line, lax.rem(other, SUBS)))
    barrier = pltpu.get_barrier_semaphore()
    everybody = targets + [t for _, t in level_targets] + first_targets + second_targets
    for device in everybody:
        pl.semaphore_signal(barrier, inc=1, device_id=device, device_id_type=MESH)
    load.wait()
    pl.semaphore_wait(barrier, len(everybody))

    def rows(index, q):
        return pl.ds(pl.multiple_of(index * ROWS + q * PART, PART), PART)

    def push(source, target, kind, q, link, device):
        pltpu.make_async_remote_copy(
            src_ref=keys.at[rows(source, q)],
            dst_ref=keys.at[rows(target, q)],
            send_sem=send.at[link],
            recv_sem=recv.at[kind, q],
            device_id=device,
            device_id_type=MESH,
        ).start()

    def await_piece(kind, q):
        ref = keys.at[pl.ds(0, PART)]
        pltpu.make_async_copy(ref, ref, recv.at[kind, q]).wait()

    UP, LOW, SUB, CORE = range(4)
    shift = 2 * core - 1

    def to_core(offset, half, kind, q):
        push(slot(offset, half), slot(offset + shift, half), kind, q, CORE, core_dev)

    def send_own(q):
        push(own_slot, slot(-2, sub), LOW_OWN, q, UP, up_dev)
        push(own_slot, slot(2, sub), UP_OWN, q, LOW, low_dev)

    def send_half(q):
        push(half_slot, slot(-2, 1 - sub), LOW_HALF, q, UP, up_dev)
        push(half_slot, slot(2, 1 - sub), UP_HALF, q, LOW, low_dev)

    def send_far(q):
        push(slot(-2, low_half), slot(-4, low_half), LOW_FAR, q, UP, up_dev)
        push(slot(2, up_half), slot(4, up_half), UP_FAR, q, LOW, low_dev)

    def got_own(q):
        await_piece(LOW_OWN, q)
        await_piece(UP_OWN, q)
        send_far(q)

    def spread_own(q):
        to_core(-2, low_half, CORE_LOW_A, q)
        to_core(2, up_half, CORE_UP_A, q)

    def got_half(q):
        await_piece(SUB_OWN, q)
        to_core(0, 1 - sub, CORE_HALF, q)

    far_offset = 4 - 8 * core
    far_half = up_far + core * (low_far - up_far)

    def got_far(q):
        await_piece(LOW_FAR, q)
        await_piece(UP_FAR, q)
        push(slot(-4, low_far), slot(-4, low_far), SUB_LOW, q, SUB, sub_dev)
        push(slot(4, up_far), slot(4, up_far), SUB_UP, q, SUB, sub_dev)
        to_core(far_offset, far_half, CORE_FAR_A, q)

    def got_near(q):
        await_piece(LOW_HALF, q)
        await_piece(UP_HALF, q)
        to_core(-2, 1 - low_half, CORE_LOW_B, q)
        to_core(2, 1 - up_half, CORE_UP_B, q)

    def got_sub(q):
        await_piece(SUB_LOW, q)
        await_piece(SUB_UP, q)
        to_core(far_offset, 1 - far_half, CORE_FAR_B, q)

    def await_all(kind):
        for q in range(CHUNKS):
            await_piece(kind, q)

    row_at = lax.broadcasted_iota(jnp.int32, (ROWS, ROWS), 0)
    column_at = lax.broadcasted_iota(jnp.int32, (ROWS, ROWS), 1)
    diagonal = row_at == column_at
    column_float = column_at.astype(jnp.float32)

    def as_column(row):
        return jnp.sum(jnp.where(diagonal, row, 0.0), axis=1, keepdims=True)

    def as_row(column):
        return jnp.sum(jnp.where(diagonal, column, 0.0), axis=0, keepdims=True)

    factor = LOG2E / math.sqrt(WIDTH)

    def score(index):
        return (
            lax.dot_general(
                keys[piece(own_slot), :], keys[piece(index), :], (((1,), (1,)), ((), ())),
                preferred_element_type=jnp.float32,
            )
            * factor
        )

    top = [None]
    total = [None]

    def absorb(index, own=False):
        tile = score(index)
        if own:
            tile = jnp.where(diagonal, LOWEST, tile)
        scores[index] = tile
        left, right = tile[:, :128], tile[:, 128:]
        high = jnp.maximum(left, right)
        if top[0] is None:
            top[0] = high
            total[0] = jnp.exp2(left - high) + jnp.exp2(right - high)
        else:
            high = jnp.maximum(high, top[0])
            total[0] = (
                total[0] * jnp.exp2(top[0] - high)
                + jnp.exp2(left - high)
                + jnp.exp2(right - high)
            )
            top[0] = high

    send_own(0)
    for q in range(CHUNKS):
        push(own_slot, own_slot, SUB_OWN, q, SUB, sub_dev)
        if q == 0:
            send_own(1)
    for q in range(CHUNKS):
        push(own_slot, slot(shift, sub), CORE_OWN, q, CORE, core_dev)

    reward_row = reward_ref[...]
    rewards[sub] = reward_row
    reward_copy = pltpu.make_async_remote_copy(
        src_ref=rewards.at[sub], dst_ref=rewards.at[sub],
        send_sem=reward_sem.at[0], recv_sem=reward_sem.at[1],
        device_id=sub_dev, device_id_type=MESH,
    )
    reward_copy.start()
    absorb(own_slot, own=True)
    reward_column = as_column(reward_row)
    partner_column = as_column((partner_ref[...] - block * BLOCK).astype(jnp.float32))
    policy_column = as_column(policy_ref[...].astype(jnp.float32))

    got_own(0)
    send_own(2)
    spread_own(0)
    got_half(0)
    await_all(CORE_OWN)
    absorb(slot(-shift, sub))

    got_own(1)
    send_own(3)
    spread_own(1)
    got_half(1)

    got_far(0)
    got_half(2)

    got_own(2)
    send_half(0)
    spread_own(2)
    got_half(3)
    absorb(half_slot)

    got_far(1)
    await_all(CORE_HALF)
    absorb(slot(-shift, 1 - sub))
    got_own(3)
    for q in range(1, CHUNKS):
        send_half(q)
    spread_own(3)
    got_sub(0)
    absorb(slot(-2, low_half))

    got_far(2)
    absorb(slot(2, up_half))
    got_near(0)
    await_all(CORE_LOW_A)
    await_all(CORE_UP_A)
    absorb(slot(-2 - shift, low_half))
    got_sub(1)
    absorb(slot(2 - shift, up_half))
    got_far(3)
    absorb(slot(-4, low_far))
    got_near(1)
    absorb(slot(4, up_far))
    got_sub(2)
    core_far = -far_offset - shift
    core_far_half = low_far + core * (up_far - low_far)
    await_all(CORE_FAR_A)
    absorb(slot(core_far, core_far_half))
    got_near(2)
    got_near(3)
    got_sub(3)
    absorb(slot(-2, 1 - low_half))
    absorb(slot(2, 1 - up_half))
    absorb(slot(-4, 1 - low_far))
    absorb(slot(4, 1 - up_far))
    await_all(CORE_LOW_B)
    absorb(slot(-2 - shift, 1 - low_half))
    await_all(CORE_UP_B)
    absorb(slot(2 - shift, 1 - up_half))
    await_all(CORE_FAR_B)
    absorb(slot(core_far, 1 - core_far_half))

    peak = jnp.max(top[0], axis=1, keepdims=True)
    summed = jnp.sum(total[0] * jnp.exp2(top[0] - peak), axis=1, keepdims=True)
    log_total = peak + jnp.log(summed) * LOG2E
    own_level = log_total - jnp.log(reward_column) * LOG2E
    level[own_slot] = as_row(own_level)
    for offset, device in level_targets:
        pltpu.make_async_remote_copy(
            src_ref=level.at[own_slot],
            dst_ref=level.at[slot(-offset, sub)],
            send_sem=level_sem.at[0],
            recv_sem=level_sem.at[1],
            device_id=device,
            device_id_type=MESH,
        ).start()

    own_match = column_float + (sub * ROWS).astype(jnp.float32) == partner_column
    half_match = column_float + ((1 - sub) * ROWS).astype(jnp.float32) == partner_column
    positive = jnp.sum(
        jnp.where(own_match, scores[own_slot], 0.0)
        + jnp.where(half_match, scores[half_slot], 0.0),
        axis=1, keepdims=True,
    )
    weighted = reward_column * ((log_total - positive) * LN2)
    weighted_ref[...] = as_row(weighted)
    labels = lax.broadcasted_iota(jnp.int32, (ROWS, 128), 1).astype(jnp.float32)
    first_sum[line] = jnp.sum(
        jnp.where(labels == policy_column, weighted, 0.0), axis=0, keepdims=True
    )
    for device in first_targets:
        pltpu.make_async_remote_copy(
            src_ref=first_sum.at[line], dst_ref=first_sum.at[line],
            send_sem=sum_sem.at[0], recv_sem=sum_sem.at[1],
            device_id=device, device_id_type=MESH,
        ).start()

    def await_rows(ref, count, sem):
        part = ref.at[pl.ds(0, count)]
        pltpu.make_async_copy(part, part, sem).wait()

    await_rows(level, SLOTS - 1, level_sem.at[1])
    reward_copy.wait()

    for index in range(SLOTS):
        tile = scores[index]
        value = jnp.exp2(tile - own_level) + jnp.exp2(tile - level[index])
        half = index - slot(0, 0)
        if 0 <= half < SUBS:
            match = column_float + float(half * ROWS) == partner_column
            value = value - jnp.where(match, reward_column + rewards[half], 0.0)
        weights[:, index * ROWS : (index + 1) * ROWS] = value.astype(jnp.bfloat16)

    await_rows(first_sum, GROUP - 1, sum_sem.at[1])
    second_sum[plane] = jnp.sum(first_sum[...], axis=0)
    for device in second_targets:
        pltpu.make_async_remote_copy(
            src_ref=second_sum.at[plane], dst_ref=second_sum.at[plane],
            send_sem=sum_sem.at[2], recv_sem=sum_sem.at[3],
            device_id=device, device_id_type=MESH,
        ).start()

    for tile in range(WIDTH // TILE):
        columns = pl.ds(tile * TILE, TILE)
        gradient_ref[:, columns] = jnp.dot(
            weights[...], keys[:, columns], preferred_element_type=jnp.float32
        )

    await_rows(second_sum, GROUP - 1, sum_sem.at[3])
    loss_ref[...] = jnp.sum(second_sum[...], axis=0) * (POLICIES / (LOOP * BLOCK))

    await_rows(level, SLOTS - 1, level_sem.at[0])
    await_rows(first_sum, GROUP - 1, sum_sem.at[0])
    await_rows(second_sum, GROUP - 1, sum_sem.at[2])
    for link, pieces in ((UP, 3), (LOW, 3), (SUB, 3), (CORE, 8)):
        part = keys.at[pl.ds(0, pieces * ROWS)]
        pltpu.make_async_copy(part, part, send.at[link]).wait()


def body(embeddings, reward, partner, policy):
    vmem = pl.BlockSpec(memory_space=pltpu.VMEM)
    weighted, gradient, loss = pl.pallas_call(
        kernel,
        out_shape=(
            jax.ShapeDtypeStruct((1, ROWS), jnp.float32),
            jax.ShapeDtypeStruct((ROWS, WIDTH), jnp.float32),
            jax.ShapeDtypeStruct((1, 128), jnp.float32),
        ),
        in_specs=[pl.BlockSpec(memory_space=pl.ANY), vmem, vmem, vmem],
        out_specs=(vmem, vmem, vmem),
        scratch_shapes=[
            pltpu.VMEM((SLOTS * ROWS, WIDTH), jnp.bfloat16),
            pltpu.VMEM((SLOTS, ROWS, ROWS), jnp.float32),
            pltpu.VMEM((ROWS, SLOTS * ROWS), jnp.bfloat16),
            pltpu.VMEM((SLOTS, 1, ROWS), jnp.float32),
            pltpu.VMEM((SUBS, 1, ROWS), jnp.float32),
            pltpu.VMEM((GROUP, 1, 128), jnp.float32),
            pltpu.VMEM((GROUP, 1, 128), jnp.float32),
            pltpu.SemaphoreType.DMA((CLASSES, CHUNKS)),
            pltpu.SemaphoreType.DMA((4,)),
            pltpu.SemaphoreType.DMA((2,)),
            pltpu.SemaphoreType.DMA((4,)),
            pltpu.SemaphoreType.DMA((2,)),
            pltpu.SemaphoreType.DMA,
        ],
        name="band",
        compiler_params=pltpu.CompilerParams(
            collective_id=0, has_side_effects=True, vmem_limit_bytes=48 * 2**20
        ),
    )(
        embeddings,
        reward.reshape(1, ROWS),
        partner.reshape(1, ROWS),
        policy.reshape(1, ROWS),
    )
    return weighted.reshape(ROWS), gradient, loss[0, :POLICIES]


def solution(mesh):
    rows = P(("loop", "sub"))
    matrix = P(("loop", "sub"), None)
    return jax.shard_map(
        body, mesh=mesh, in_specs=(matrix, rows, rows, rows),
        out_specs=(rows, matrix, P()), check_vma=False,
    )
```

time: 290 us -> 68.3 us (0.24)
  waiting for transfers between devices: 143 us -> 0 us
  blocking collectives: 79.7 us -> 0 us
  Pallas kernels: 0 us -> 63.8 us
  starting transfers between devices: 27.3 us -> 0 us
  matrix products: 14.1 us -> 0 us
  between operations: 14.3 us -> 0.67 us
  local copies, waits for them, and re-layouts: 9.46 us -> 3.77 us
    ppermute x16 -> x0, waiting for transfers between devices: 110 us -> none  [passed_along(): return lax.ppermute(value, axis, pairs)]
    psum x1 -> x0, blocking collectives: 75.9 us -> none  [body(): lax.psum(partial_sum, ('loop', 'sub'))]
    pallas_call x0 -> x1, Pallas kernels: none -> 63.8 us  [body(): pl.pallas_call(kernel, out_shape=(jax.ShapeDtypeStruct((1, ROWS), jnp.flo...]
    all_gather x1 -> x0, waiting for transfers between devices: 32.1 us -> none  [body(): local_block = lax.all_gather(embeddings, 'sub', axis=0, tiled=True)]
    ppermute x16 -> x0, starting transfers between devices: 27.3 us -> none  [passed_along(): return lax.ppermute(value, axis, pairs)]
    dot_general x18 -> x0, matrix products: 14.1 us -> none  [the longest x9 7.8 us: body(): jnp.dot(coefficient.astype(jnp.bfloat16), key_blocks[number], preferred_e...]
    unnamed x58 -> x10, local copies, waits for them, and re-layouts: 9.41 us -> 3.26 us
    all_gather x1 -> x0, blocking collectives: 3.74 us -> none  [body(): local_stats = lax.all_gather(own_stats, 'sub', axis=1, tiled=True)]
  transfers between devices with their start and end apart: 17 -> 0, of which waited for: 8 -> 0; matrix products, arithmetic and copies ran while one was open for 3% -> 0% of each run, Pallas kernels for 0% -> 0%
where the time goes in v1:
time: 68.3 us; the launch traced here: 68.2 us
  Pallas kernels  63.8 us (93%)
  local copies, waits for them, and re-layouts  3.77 us (6%)
    pallas_call x1, Pallas kernels, body(): pl.pallas_call(kernel, out_shape=(jax.ShapeDtypeStruct((1, ROWS), jnp.flo...  63.8 us
    unnamed x10, local copies, waits for them, and re-layouts  3.26 us

profile of v1, /device:TPU:1, one launch (start us, length us, event | category | flops | bytes accessed | tf_op | source)
XLA Modules:
  0.0 68.2 jit_solution(3635025344657655745)
XLA Ops:
  0.6 0.0 copy-start.2
  0.6 0.0 copy-start.3
  0.7 0.0 copy-start.1
  0.7 0.7 copy-done.2
  1.3 0.0 copy-done.3
  1.3 0.0 copy-done.1
  1.3 0.0 copy-start
  1.3 1.0 %copy-done = bf16[256,1024]{1,0:T(8,128)(2,1)S(1)} copy-done((bf16[256,1024]{1,0:T(8,128)(2,1)S(1)}, bf16[256,1024]{1,0:T(8,128)(2,1)}, u32[]{:S(2)}) %copy-start) | copy-done | bytes 524312
  2.4 63.8 %band.1 = (f32[1,256]{1,0:T(1,128)S(1)}, f32[256,1024]{1,0:T(8,128)S(1)}, f32[1,128]{1,0:T(1,128)S(1)}) custom-call(bf16[256,1024]{1,0:T(8,128)(2,1)S(1)} %copy-done, f32[1,256]{1,0:T(1,128)S(1)} %bitcast.6, s32[1,256]{1,0:T(1,128)S(1)} %bitcast.7, s32[1,256]{1,0:T(1,128)S(1)} %bitcast.8), custom_call_target="tpu_custom_call" | custom-call | tf_op jit(solution)/shard_map/band/pallas_call | solution.py:380
  66.2 0.5 slice_bitcast_fusion
  66.7 0.6 copy.9
  67.2 1.0 %copy.10 = f32[256,1024]{1,0:T(8,128)} copy(f32[256,1024]{1,0:T(8,128)S(1)} %get-tuple-element.13) | data formatting | bytes 2097152
Async XLA Ops:
  0.6 0.7 copy-start.2
  0.6 0.7 %copy-start.3 = (s32[256]{0:T(256)S(1)}, s32[256]{0:T(256)}, u32[]{:S(2)}) copy-start(s32[256]{0:T(256)} %param.7) | copy-start | bytes 3076
  0.7 0.7 %copy-start.1 = (f32[256]{0:T(256)S(1)}, f32[256]{0:T(256)}, u32[]{:S(2)}) copy-start(f32[256]{0:T(256)} %param.5) | copy-start | bytes 3076
  1.3 1.0 %copy-start = (bf16[256,1024]{1,0:T(8,128)(2,1)S(1)}, bf16[256,1024]{1,0:T(8,128)(2,1)}, u32[]{:S(2)}) copy-start(bf16[256,1024]{1,0:T(8,128)(2,1)} %x_ref.1) | copy-start | bytes 1572868

commit v2 on v1

v2 whole, which is shorter than its diff:
```python
import functools
import math

import jax
import jax.numpy as jnp
from jax import lax
from jax.experimental import pallas as pl
from jax.experimental.pallas import tpu as pltpu
from jax.sharding import PartitionSpec as P

RADIUS = 4
POLICIES = 16
ROWS = 256
WIDTH = 1024
SUBS = 2
BLOCK = ROWS * SUBS
LOOP = 128
SEAM = 64
CHUNKS = 8
LINE = 8
MOVED = 2
SPAN = 3
LEVELS = 2 * RADIUS + 1
PIECES = 4
PART = ROWS // CHUNKS
SLOTS = (2 * RADIUS + 1) * SUBS
GROUP = 16
LOG2E = 1.4426950408889634
LN2 = 0.6931471805599453
LOWEST = -1e30
MESH = pl.DeviceIdType.MESH

OWN, HALF, FAR, SUB_FAR = 0, 2, 4, 6
CORE_NEAR_A, CORE_NEAR_B = 8, 10
SUB_OWN, CORE_OWN, CORE_HALF, CORE_FAR_A, CORE_FAR_B = 12, 13, 14, 15, 16
CLASSES = 17


def slot(offset, half):
    return (offset + RADIUS) * SUBS + half


def kernel(
    x_ref, reward_ref, partner_ref, policy_ref,
    weighted_ref, gradient_ref, loss_ref,
    keys, scores, shares, level, rewards, integers, first_sum, second_sum,
    recv, send, level_sem, sum_sem, reward_sem, local_sem,
):
    block = lax.axis_index("loop")
    sub = lax.axis_index("sub")
    core = lax.rem(block, 2)

    def crosses(at):
        return jnp.where(lax.rem(at, SEAM) >= SEAM - 2, 1, 0)

    def flip(half, by):
        return half + by - 2 * half * by

    def at_loop(index):
        return lax.rem(index + LOOP, LOOP)

    cross_up = crosses(block)
    cross_low = crosses(at_loop(block - 2))
    cross_up2 = crosses(at_loop(block + 2))
    cross_low2 = crosses(at_loop(block - 4))
    up_dev = (at_loop(block + 2), flip(sub, cross_up))
    low_dev = (at_loop(block - 2), flip(sub, cross_low))
    sub_dev = (block, 1 - sub)
    core_dev = (block + 1 - 2 * core, sub)
    low_half = flip(sub, cross_low)
    up_half = flip(sub, cross_up)
    low_far = flip(low_half, cross_low2)
    up_far = flip(up_half, cross_up2)

    own_slot = slot(0, sub)
    half_slot = slot(0, 1 - sub)

    def piece(index):
        return pl.ds(pl.multiple_of(index * ROWS, ROWS), ROWS)

    loads = [
        pltpu.make_async_copy(x_ref, keys.at[piece(own_slot)], local_sem.at[0]),
        pltpu.make_async_copy(reward_ref, rewards.at[sub], local_sem.at[1]),
        pltpu.make_async_copy(partner_ref, integers.at[0], local_sem.at[2]),
        pltpu.make_async_copy(policy_ref, integers.at[1], local_sem.at[3]),
    ]
    for load in loads:
        load.start()

    level_targets = []
    for offset in sorted(range(-RADIUS, RADIUS + 1), key=lambda k: (k % 2, abs(k))):
        for other in range(SUBS):
            if offset == 0 and other == 0:
                continue
            level_targets.append((offset, (at_loop(block + offset), flip(sub, other))))
    line = lax.rem(block, GROUP)
    line_base = block - line
    first_targets = [(line_base + lax.rem(line + i, GROUP), sub) for i in range(1, GROUP)]
    plane = (block // GROUP) * SUBS + sub
    second_targets = []
    for i in range(1, GROUP):
        other = lax.rem(plane + i, GROUP)
        second_targets.append(((other // SUBS) * GROUP + line, lax.rem(other, SUBS)))
    barrier = pltpu.get_barrier_semaphore()
    everybody = [t for _, t in level_targets] + first_targets + second_targets
    for device in everybody:
        pl.semaphore_signal(barrier, inc=1, device_id=device, device_id_type=MESH)
    for load in loads:
        load.wait()
    pl.semaphore_wait(barrier, len(everybody))

    def rows(index, q):
        return pl.ds(pl.multiple_of(index * ROWS + q * PART, PART), PART)

    def push(source, target, kind, q, link, device):
        pltpu.make_async_remote_copy(
            src_ref=keys.at[rows(source, q)],
            dst_ref=keys.at[rows(target, q)],
            send_sem=send.at[link],
            recv_sem=recv.at[kind, q],
            device_id=device,
            device_id_type=MESH,
        ).start()

    def await_piece(kind, q):
        ref = keys.at[pl.ds(0, PART)]
        pltpu.make_async_copy(ref, ref, recv.at[kind, q]).wait()

    SUB, CORE = 2, 3
    shift = 2 * core - 1

    z = lax.rem(block // 2, LINE)
    side_b = jnp.where(z >= LINE // 2, 1, 0)
    side_a = 1 - side_b
    edge = jnp.where(jnp.logical_or(z < 2, z >= LINE - 2), 1, 0)

    def pick(side, low, up):
        return low + side * (up - low)

    def near(side):
        return 4 * side - 2

    def device_of(side):
        return tuple(pick(side, low, up) for low, up in zip(low_dev, up_dev))

    def near_half(side):
        return pick(side, low_half, up_half)

    def far_half_of(side):
        return pick(side, low_far, up_far)

    def to_core(offset, half, kind, q):
        push(slot(offset, half), slot(offset + shift, half), kind, q, CORE, core_dev)

    def send_own(side, *chunks):
        for q in chunks:
            push(own_slot, slot(-near(side), sub), OWN + 1 - side, q, side, device_of(side))

    def send_half(side, *chunks):
        for q in chunks:
            push(
                half_slot, slot(-near(side), 1 - sub), HALF + 1 - side, q, side,
                device_of(side),
            )

    def got_own(side, q):
        other = 1 - side
        await_piece(OWN + side, q)
        half = near_half(side)
        push(
            slot(near(side), half), slot(-2 * near(other), half), FAR + side, q, other,
            device_of(other),
        )

    def spread_own(side, q):
        to_core(near(side), near_half(side), CORE_NEAR_A + side, q)

    def got_half(q):
        await_piece(SUB_OWN, q)
        to_core(0, 1 - sub, CORE_HALF, q)

    far_offset = 4 - 8 * core
    far_half = far_half_of(1 - core)

    def got_far(side, q):
        await_piece(FAR + side, q)
        at = slot(2 * near(side), far_half_of(side))
        push(at, at, SUB_FAR + side, q, SUB, sub_dev)

    def spread_far(q):
        to_core(far_offset, far_half, CORE_FAR_A, q)

    def got_near(side, q):
        await_piece(HALF + side, q)
        to_core(near(side), 1 - near_half(side), CORE_NEAR_B + side, q)

    def got_sub(q):
        await_piece(SUB_FAR, q)
        await_piece(SUB_FAR + 1, q)
        to_core(far_offset, 1 - far_half, CORE_FAR_B, q)

    def await_all(kind):
        for q in range(CHUNKS):
            await_piece(kind, q)

    row_at = lax.broadcasted_iota(jnp.int32, (ROWS, ROWS), 0)
    column_at = lax.broadcasted_iota(jnp.int32, (ROWS, ROWS), 1)
    diagonal = row_at == column_at
    column_float = column_at.astype(jnp.float32)

    def as_column(row):
        return jnp.sum(jnp.where(diagonal, row, 0.0), axis=1, keepdims=True)

    def as_row(column):
        return jnp.sum(jnp.where(diagonal, column, 0.0), axis=0, keepdims=True)

    factor = LOG2E / math.sqrt(WIDTH)

    top = [None]
    total = [None]

    def absorb(index, part=None, own=False):
        absorb_all([index], part, own)

    def absorb_all(indices, part=None, own=False):
        first, count = (0, ROWS) if part is None else (part * 128, 128)
        parts = []
        for index in indices:
            block_rows = pl.ds(pl.multiple_of(index * ROWS + first, 128), count)
            tile = lax.dot_general(
                keys[piece(own_slot), :], keys[block_rows, :], (((1,), (1,)), ((), ())),
                preferred_element_type=jnp.float32,
            ) * factor
            if own:
                tile = jnp.where(diagonal, LOWEST, tile)
            scores[index, :, first : first + count] = tile
            parts += [tile[:, i : i + 128] for i in range(0, count, 128)]
        high = functools.reduce(jnp.maximum, parts)
        if top[0] is not None:
            high = jnp.maximum(high, top[0])
        fresh = functools.reduce(jnp.add, [jnp.exp2(t - high) for t in parts])
        if top[0] is not None:
            fresh = fresh + total[0] * jnp.exp2(top[0] - high)
        top[0], total[0] = high, fresh

    for q in range(4):
        send_own(side_a, q)
        send_own(side_b, q)
        push(own_slot, own_slot, SUB_OWN, q, SUB, sub_dev)

    @pl.when(edge == 1)
    def _():
        send_own(side_a, 4, 5)

    for q in range(4, CHUNKS):
        push(own_slot, own_slot, SUB_OWN, q, SUB, sub_dev)

    def near_a(q):
        got_own(side_a, q)
        if q < 4:
            send_own(side_b, q + 4)
        elif q < 7:
            send_half(side_b, q - 4)
        else:
            send_half(side_b, *range(3, CHUNKS - MOVED))

            @pl.when(z != 0)
            def _():
                send_half(side_b, *range(CHUNKS - MOVED, CHUNKS))
        spread_own(side_a, q)

    def near_b(q):
        got_own(side_b, q)
        if q < 2:
            send_own(side_a, q + 4 + 2 * edge)
        elif q < 4:

            @pl.when(edge == 1)
            def _():
                send_half(side_a, q - 2)

            @pl.when(edge == 0)
            def _():
                send_own(side_a, q + 4)
        else:
            send_half(side_a, q - 4 + 2 * edge)
        if q == 7:

            @pl.when(edge == 0)
            def _():
                send_half(side_a, 4, 5)

            send_half(side_a, 6, 7)
        if q >= CHUNKS - MOVED:
            at = slot(near(side_b), near_half(side_b))

            @pl.when(z == LINE - 1)
            def _():
                push(at, at, HALF + side_b, q, SUB, sub_dev)
        spread_own(side_b, q)

    def far_a(q):
        got_far(side_a, q)

    def far_b(q):
        got_far(side_b, q)
        spread_far(q)

    near_a(0)
    for q in range(CHUNKS):
        push(own_slot, slot(shift, sub), CORE_OWN, q, CORE, core_dev)
    reward_copy = pltpu.make_async_remote_copy(
        src_ref=rewards.at[sub], dst_ref=rewards.at[sub],
        send_sem=reward_sem.at[0], recv_sem=reward_sem.at[1],
        device_id=sub_dev, device_id_type=MESH,
    )
    reward_copy.start()
    near_a(1)
    absorb(own_slot, own=True)
    near_a(2)
    near_b(0)
    near_a(3)
    near_b(1)
    far_a(0)
    for q in range(3):
        got_half(q)
    near_b(2)
    near_a(4)
    near_b(3)
    far_a(1)
    await_all(CORE_OWN)
    absorb(slot(-shift, sub))
    near_a(5)
    far_b(0)
    far_a(2)
    for q in range(3, CHUNKS):
        got_half(q)
    near_b(4)
    near_a(6)
    far_b(1)
    near_b(5)
    far_a(3)
    absorb(half_slot)
    near_a(7)
    far_b(2)
    near_b(6)
    far_a(4)
    reward_row = rewards[sub]
    reward_column = as_column(reward_row)
    partner_column = as_column((integers[0] - block * BLOCK).astype(jnp.float32))
    policy_column = as_column(integers[1].astype(jnp.float32))
    log_reward = jnp.log(reward_column) * LOG2E
    absorb(slot(near(side_a), near_half(side_a)))
    far_b(3)
    near_b(7)
    far_a(5)
    await_all(CORE_HALF)
    absorb(slot(-shift, 1 - sub))
    absorb(slot(near(side_b), near_half(side_b)))
    far_b(4)
    await_all(CORE_NEAR_A + side_a)
    absorb(slot(near(side_a) - shift, near_half(side_a)))
    far_a(6)
    await_all(CORE_NEAR_A + side_b)
    absorb(slot(near(side_b) - shift, near_half(side_b)))
    own_match = column_float + (sub * ROWS).astype(jnp.float32) == partner_column
    half_match = column_float + ((1 - sub) * ROWS).astype(jnp.float32) == partner_column
    positive = jnp.sum(
        jnp.where(own_match, scores[own_slot], 0.0)
        + jnp.where(half_match, scores[half_slot], 0.0),
        axis=1, keepdims=True,
    )
    far_b(5)
    absorb(slot(2 * near(side_a), far_half_of(side_a)), 0)
    far_a(7)
    absorb(slot(2 * near(side_b), far_half_of(side_b)), 0)
    for q in range(3):
        got_sub(q)
        got_near(side_a, q)
        got_near(side_b, q)
    far_b(6)
    absorb(slot(2 * near(side_a), far_half_of(side_a)), 1)
    core_far = -far_offset - shift
    core_far_half = far_half_of(core)
    got_sub(3)
    got_near(side_a, 3)
    got_near(side_b, 3)
    far_b(7)

    def await_some(kind, part):
        for q in range(part * CHUNKS // 2, (part + 1) * CHUNKS // 2):
            await_piece(kind, q)

    def rest(part):
        sides = (side_a, side_b)
        absorb_all(
            [slot(near(side), 1 - near_half(side)) for side in sides]
            + [slot(2 * near(side), 1 - far_half_of(side)) for side in sides],
            part,
        )
        for side in sides:
            await_some(CORE_NEAR_B + side, part)
        await_some(CORE_FAR_B, part)
        absorb_all(
            [slot(near(side) - shift, 1 - near_half(side)) for side in sides]
            + [slot(core_far, 1 - core_far_half)],
            part,
        )

    rest(0)
    absorb(slot(2 * near(side_b), far_half_of(side_b)), 1)
    await_all(CORE_FAR_A)
    absorb(slot(core_far, core_far_half))
    for q in range(4, CHUNKS):
        got_near(side_a, q)
        got_near(side_b, q)
        got_sub(q)
    rest(1)

    peak = jnp.max(top[0], axis=1, keepdims=True)
    summed = jnp.sum(total[0] * jnp.exp2(top[0] - peak), axis=1, keepdims=True)
    log_total = peak + jnp.log(summed) * LOG2E
    weighted = reward_column * ((log_total - positive) * LN2)
    labels = lax.broadcasted_iota(jnp.int32, (ROWS, 128), 1).astype(jnp.float32)
    first_sum[line] = jnp.sum(
        jnp.where(labels == policy_column, weighted, 0.0), axis=0, keepdims=True
    )
    for device in first_targets:
        pltpu.make_async_remote_copy(
            src_ref=first_sum.at[line], dst_ref=first_sum.at[line],
            send_sem=sum_sem.at[0], recv_sem=sum_sem.at[1],
            device_id=device, device_id_type=MESH,
        ).start()
    own_level = log_total - log_reward
    level[own_slot] = as_row(own_level)
    for offset, device in sorted(level_targets, key=lambda entry: -abs(entry[0])):
        pltpu.make_async_remote_copy(
            src_ref=level.at[own_slot],
            dst_ref=level.at[slot(-offset, sub)],
            send_sem=level_sem.at[LEVELS],
            recv_sem=level_sem.at[RADIUS - offset],
            device_id=device,
            device_id_type=MESH,
        ).start()
    weighted_ref[...] = as_row(weighted)

    reward_copy.wait()
    for index in range(SLOTS):
        half = index - slot(0, 0)
        value = jnp.exp2(scores[index] - own_level)
        if 0 <= half < SUBS:
            match = column_float + float(half * ROWS) == partner_column
            value = value - jnp.where(match, reward_column + rewards[half], 0.0)
        shares[index] = value

    def await_rows(ref, count, sem):
        part = ref.at[pl.ds(0, count)]
        pltpu.make_async_copy(part, part, sem).wait()

    await_rows(first_sum, GROUP - 1, sum_sem.at[1])
    second_sum[plane] = jnp.sum(first_sum[...], axis=0)
    for device in second_targets:
        pltpu.make_async_remote_copy(
            src_ref=second_sum.at[plane], dst_ref=second_sum.at[plane],
            send_sem=sum_sem.at[2], recv_sem=sum_sem.at[3],
            device_id=device, device_id_type=MESH,
        ).start()
    toward_a = 2 * side_a - 1
    offsets = [0] + [toward_a * k for k in range(1, RADIUS + 1)]
    offsets += [-toward_a * k for k in range(1, RADIUS + 1)]
    for begin in range(0, LEVELS, SPAN):
        group = offsets[begin : begin + SPAN]
        for number, offset in enumerate(group):
            await_rows(level, SUBS - (begin + number == 0), level_sem.at[RADIUS + offset])
        product = None
        for offset in group:
            values = []
            for half in range(SUBS):
                index = slot(offset, half)
                value = shares[index] + jnp.exp2(scores[index] - level[index])
                values.append(value.astype(jnp.bfloat16))
            term = jnp.dot(
                jnp.concatenate(values, axis=1),
                keys[pl.ds(pl.multiple_of(slot(offset, 0) * ROWS, BLOCK), BLOCK), :],
                preferred_element_type=jnp.float32,
            )
            product = term if product is None else product + term
        gradient_ref[...] = product if begin == 0 else gradient_ref[...] + product

    await_rows(second_sum, GROUP - 1, sum_sem.at[3])
    loss = jnp.sum(second_sum[...], axis=0) * (POLICIES / (LOOP * BLOCK))
    loss_ref[...] = loss[:, :POLICIES]

    await_rows(level, SLOTS - 1, level_sem.at[LEVELS])
    await_rows(first_sum, GROUP - 1, sum_sem.at[0])
    await_rows(second_sum, GROUP - 1, sum_sem.at[2])
    def await_sent(link, count):
        part = keys.at[pl.ds(0, count)]
        pltpu.make_async_copy(part, part, send.at[link]).wait()

    moved = MOVED * PART
    await_sent(side_a, 3 * ROWS)
    await_sent(side_b, 3 * ROWS - moved)
    await_sent(SUB, 3 * ROWS)
    await_sent(CORE, 8 * ROWS)

    @pl.when(z != 0)
    def _():
        await_sent(side_b, moved)

    @pl.when(z == LINE - 1)
    def _():
        await_sent(SUB, moved)


def finish(a_ref, b_ref, c_ref, a_out, b_out, c_out, sems):
    step = ROWS // PIECES
    pairs = [(b_ref.at[r], b_out.at[r]) for r in (pl.ds(i * step, step) for i in range(PIECES))]
    pairs += [(a_ref, a_out), (c_ref, c_out)]
    copies = [pltpu.make_async_copy(p, q, sems.at[i]) for i, (p, q) in enumerate(pairs)]
    for copy in copies:
        copy.start()
    for copy in copies:
        copy.wait()


def body(embeddings, reward, partner, policy):
    vmem = pl.BlockSpec(memory_space=pltpu.VMEM)
    hbm = pl.BlockSpec(memory_space=pltpu.HBM)
    outs = (
        jax.ShapeDtypeStruct((1, ROWS), jnp.float32),
        jax.ShapeDtypeStruct((ROWS, WIDTH), jnp.float32),
        jax.ShapeDtypeStruct((1, POLICIES), jnp.float32),
    )
    results = pl.pallas_call(
        kernel,
        out_shape=outs,
        in_specs=[hbm, hbm, hbm, hbm],
        out_specs=(vmem, vmem, vmem),
        scratch_shapes=[
            pltpu.VMEM((SLOTS * ROWS, WIDTH), jnp.bfloat16),
            pltpu.VMEM((SLOTS, ROWS, ROWS), jnp.float32),
            pltpu.VMEM((SLOTS, ROWS, ROWS), jnp.float32),
            pltpu.VMEM((SLOTS, 1, ROWS), jnp.float32),
            pltpu.VMEM((SUBS, 1, ROWS), jnp.float32),
            pltpu.VMEM((2, 1, ROWS), jnp.int32),
            pltpu.VMEM((GROUP, 1, 128), jnp.float32),
            pltpu.VMEM((GROUP, 1, 128), jnp.float32),
            pltpu.SemaphoreType.DMA((CLASSES, CHUNKS)),
            pltpu.SemaphoreType.DMA((4,)),
            pltpu.SemaphoreType.DMA((LEVELS + 1,)),
            pltpu.SemaphoreType.DMA((4,)),
            pltpu.SemaphoreType.DMA((2,)),
            pltpu.SemaphoreType.DMA((4,)),
        ],
        name="band",
        compiler_params=pltpu.CompilerParams(
            collective_id=0, has_side_effects=True, vmem_limit_bytes=48 * 2**20
        ),
    )(
        *(
            pltpu.with_memory_space_constraint(a, pltpu.HBM)
            for a in (
                embeddings, reward.reshape(1, ROWS), partner.reshape(1, ROWS), policy.reshape(1, ROWS)
            )
        )
    )
    weighted, gradient, loss = pl.pallas_call(
        finish,
        out_shape=outs,
        in_specs=[vmem, vmem, vmem],
        out_specs=(hbm, hbm, hbm),
        scratch_shapes=[pltpu.SemaphoreType.DMA((PIECES + 2,))],
        name="finish",
        compiler_params=pltpu.CompilerParams(vmem_limit_bytes=8 * 2**20),
    )(*results)
    return weighted.reshape(ROWS), gradient, loss.reshape(POLICIES)


def solution(mesh):
    rows = P(("loop", "sub"))
    matrix = P(("loop", "sub"), None)
    return jax.shard_map(
        body, mesh=mesh, in_specs=(matrix, rows, rows, rows),
        out_specs=(rows, matrix, P()), check_vma=False,
    )
```

time: 68.3 us -> 61.4 us (0.90)
  local copies, waits for them, and re-layouts: 3.77 us -> 0 us
  Pallas kernels: 63.8 us -> 60.6 us
    unnamed x10 -> x0, local copies, waits for them, and re-layouts: 3.26 us -> none
    pallas_call x1 -> x2, Pallas kernels: 63.8 us -> 60.6 us  [the longest x1 59.6 us: body(): pl.pallas_call(kernel, out_shape=outs, in_specs=[hbm, hbm, hbm, hbm], out...]
where the time goes in v2:
time: 61.4 us; the launch traced here: 61.3 us
  Pallas kernels  60.6 us (99%)
  between operations  0.64 us (1%)
    pallas_call x1, Pallas kernels, body(): pl.pallas_call(kernel, out_shape=outs, in_specs=[hbm, hbm, hbm, hbm], out...  59.6 us

profile of v2, /device:TPU:1, one launch (start us, length us, event | category | flops | bytes accessed | tf_op | source)
XLA Modules:
  0.0 61.3 jit_solution(10890537793859905014)
XLA Ops:
  0.6 59.6 %band.1 = (f32[1,256]{1,0:T(1,128)S(1)}, f32[256,1024]{1,0:T(8,128)S(1)}, f32[1,16]{1,0:T(1,128)S(1)}) custom-call(bf16[256,1024]{1,0:T(8,128)(2,1)} %x_ref.1, f32[1,256]{1,0:T(1,128)} %bitcast.5, s32[1,256]{1,0:T(1,128)} %bitcast.6, s32[1,256]{1,0:T(1,128)} %bitcast.7), custom_call_target="tpu_custom_call" | custom-call | tf_op jit(solution)/shard_map/band/pallas_call | solution.py:535
  60.3 1.0 %finish.1 = (f32[1,256]{1,0:T(1,128)}, f32[256,1024]{1,0:T(8,128)}, f32[1,16]{1,0:T(1,128)}) custom-call(f32[1,256]{1,0:T(1,128)S(1)} %get-tuple-element.9.a_ref, f32[256,1024]{1,0:T(8,128)S(1)} %get-tuple-element.10.b_ref, f32[1,16]{1,0:T(1,128)S(1)} %get-tuple-element.11.c_ref), custom_call_target="tpu_custom_call" | custom-call | tf_op jit(solution)/shard_map/finish/pallas_call | solution.py:568

commit v3 on v2

--- a/solution.py
+++ b/solution.py
@@ -21,6 +21,7 @@
 MOVED = 2
 SPAN = 3
 LEVELS = 2 * RADIUS + 1
+TURNS = 4
 PIECES = 4
 PART = ROWS // CHUNKS
 SLOTS = (2 * RADIUS + 1) * SUBS
@@ -44,7 +45,7 @@
     x_ref, reward_ref, partner_ref, policy_ref,
     weighted_ref, gradient_ref, loss_ref,
     keys, scores, shares, level, rewards, integers, first_sum, second_sum,
-    recv, send, level_sem, sum_sem, reward_sem, local_sem,
+    recv, send, level_sem, sum_sem, reward_sem, local_sem, word_sem,
 ):
     block = lax.axis_index("loop")
     sub = lax.axis_index("sub")
@@ -95,19 +96,39 @@
             level_targets.append((offset, (at_loop(block + offset), flip(sub, other))))
     line = lax.rem(block, GROUP)
     line_base = block - line
-    first_targets = [(line_base + lax.rem(line + i, GROUP), sub) for i in range(1, GROUP)]
+    farthest = sorted(range(1, GROUP), key=lambda i: -min(i, GROUP - i))
+    first_targets = [(line_base + lax.rem(line + i, GROUP), sub) for i in farthest]
     plane = (block // GROUP) * SUBS + sub
     second_targets = []
-    for i in range(1, GROUP):
+    for i in farthest:
         other = lax.rem(plane + i, GROUP)
         second_targets.append(((other // SUBS) * GROUP + line, lax.rem(other, SUBS)))
     barrier = pltpu.get_barrier_semaphore()
-    everybody = [t for _, t in level_targets] + first_targets + second_targets
-    for device in everybody:
+    x_base = block - lax.rem(block, SEAM)
+    beside = [
+        core_dev,
+        sub_dev,
+        (at_loop(block + SEAM), 1 - sub),
+        (line_base + lax.rem(line + 2, GROUP), sub),
+        (line_base + lax.rem(line + GROUP - 2, GROUP), sub),
+        (x_base + lax.rem(block + GROUP, SEAM), sub),
+        (x_base + lax.rem(block + SEAM - GROUP, SEAM), sub),
+    ]
+    greeted = [low_dev, up_dev] + beside
+    for device in greeted:
         pl.semaphore_signal(barrier, inc=1, device_id=device, device_id_type=MESH)
     for load in loads:
         load.wait()
-    pl.semaphore_wait(barrier, len(everybody))
+    pl.semaphore_wait(barrier, len(greeted))
+
+    def tell(turn):
+        for device in beside:
+            pl.semaphore_signal(
+                word_sem.at[turn], inc=1, device_id=device, device_id_type=MESH
+            )
+
+    def hear(turn):
+        pl.semaphore_wait(word_sem.at[turn], len(beside))
 
     def rows(index, q):
         return pl.ds(pl.multiple_of(index * ROWS + q * PART, PART), PART)
@@ -316,6 +337,7 @@
     )
     reward_copy.start()
     near_a(1)
+    tell(0)
     absorb(own_slot, own=True)
     near_a(2)
     near_b(0)
@@ -328,6 +350,8 @@
     near_a(4)
     near_b(3)
     far_a(1)
+    hear(0)
+    tell(1)
     await_all(CORE_OWN)
     absorb(slot(-shift, sub))
     near_a(5)
@@ -343,6 +367,8 @@
     absorb(half_slot)
     near_a(7)
     far_b(2)
+    hear(1)
+    tell(2)
     near_b(6)
     far_a(4)
     reward_row = rewards[sub]
@@ -358,6 +384,8 @@
     absorb(slot(-shift, 1 - sub))
     absorb(slot(near(side_b), near_half(side_b)))
     far_b(4)
+    hear(2)
+    tell(3)
     await_all(CORE_NEAR_A + side_a)
     absorb(slot(near(side_a) - shift, near_half(side_a)))
     far_a(6)
@@ -379,6 +407,7 @@
         got_near(side_a, q)
         got_near(side_b, q)
     far_b(6)
+    hear(3)
     absorb(slot(2 * near(side_a), far_half_of(side_a)), 1)
     core_far = -far_offset - shift
     core_far_half = far_half_of(core)
@@ -552,6 +581,7 @@
             pltpu.SemaphoreType.DMA((4,)),
             pltpu.SemaphoreType.DMA((2,)),
             pltpu.SemaphoreType.DMA((4,)),
+            pltpu.SemaphoreType.REGULAR((TURNS,)),
         ],
         name="band",
         compiler_params=pltpu.CompilerParams(

time: 61.4 us -> 60.6 us (0.987)
  Pallas kernels: 60.6 us -> 59.9 us
    pallas_call x1, Pallas kernels: 59.6 us -> 58.8 us  [body(): pl.pallas_call(kernel, out_shape=outs, in_specs=[hbm, hbm, hbm, hbm], out...]
where the time goes in v3:
time: 60.6 us; the launch traced here: 60.5 us
  Pallas kernels  59.9 us (99%)
  between operations  0.64 us (1%)
    pallas_call x1, Pallas kernels, body(): pl.pallas_call(kernel, out_shape=outs, in_specs=[hbm, hbm, hbm, hbm], out...  58.8 us

profile of v3, /device:TPU:1, one launch (start us, length us, event | category | flops | bytes accessed | tf_op | source)
XLA Modules:
  0.0 60.5 jit_solution(4025756699209719569)
XLA Ops:
  0.6 58.8 %band.1 = (f32[1,256]{1,0:T(1,128)S(1)}, f32[256,1024]{1,0:T(8,128)S(1)}, f32[1,16]{1,0:T(1,128)S(1)}) custom-call(bf16[256,1024]{1,0:T(8,128)(2,1)} %x_ref.1, f32[1,256]{1,0:T(1,128)} %bitcast.5, s32[1,256]{1,0:T(1,128)} %bitcast.6, s32[1,256]{1,0:T(1,128)} %bitcast.7), custom_call_target="tpu_custom_call" | custom-call | tf_op jit(solution)/shard_map/band/pallas_call | solution.py:564
  59.5 1.0 %finish.1 = (f32[1,256]{1,0:T(1,128)}, f32[256,1024]{1,0:T(8,128)}, f32[1,16]{1,0:T(1,128)}) custom-call(f32[1,256]{1,0:T(1,128)S(1)} %get-tuple-element.9.a_ref, f32[256,1024]{1,0:T(8,128)S(1)} %get-tuple-element.10.b_ref, f32[1,16]{1,0:T(1,128)S(1)} %get-tuple-element.11.c_ref), custom_call_target="tpu_custom_call" | custom-call | tf_op jit(solution)/shard_map/finish/pallas_call | solution.py:598

commit v4 on v3

--- a/solution.py
+++ b/solution.py
@@ -19,7 +19,6 @@
 CHUNKS = 8
 LINE = 8
 MOVED = 2
-SPAN = 3
 LEVELS = 2 * RADIUS + 1
 TURNS = 4
 PIECES = 4
@@ -44,7 +43,7 @@
 def kernel(
     x_ref, reward_ref, partner_ref, policy_ref,
     weighted_ref, gradient_ref, loss_ref,
-    keys, scores, shares, level, rewards, integers, first_sum, second_sum,
+    keys, scores, level, rewards, integers, first_sum, second_sum,
     recv, send, level_sem, sum_sem, reward_sem, local_sem, word_sem,
 ):
     block = lax.axis_index("loop")
@@ -88,21 +87,20 @@
     for load in loads:
         load.start()
 
-    level_targets = []
-    for offset in sorted(range(-RADIUS, RADIUS + 1), key=lambda k: (k % 2, abs(k))):
-        for other in range(SUBS):
-            if offset == 0 and other == 0:
-                continue
-            level_targets.append((offset, (at_loop(block + offset), flip(sub, other))))
     line = lax.rem(block, GROUP)
     line_base = block - line
-    farthest = sorted(range(1, GROUP), key=lambda i: -min(i, GROUP - i))
-    first_targets = [(line_base + lax.rem(line + i, GROUP), sub) for i in farthest]
+    first_targets = [(line_base + lax.rem(line + i, GROUP), sub) for i in range(1, GROUP)]
     plane = (block // GROUP) * SUBS + sub
+    x = lax.rem(block // GROUP, 4)
+    y = (block // SEAM) * SUBS + sub
+    steps = [(dx, dy) for dx in range(4) for dy in range(4) if dx or dy]
+    steps.sort(key=lambda step: sum(min(d, 4 - d) for d in step))
     second_targets = []
-    for i in farthest:
-        other = lax.rem(plane + i, GROUP)
-        second_targets.append(((other // SUBS) * GROUP + line, lax.rem(other, SUBS)))
+    for dx, dy in steps:
+        at_x, at_y = lax.rem(x + dx, 4), lax.rem(y + dy, 4)
+        second_targets.append(
+            ((at_y // SUBS) * SEAM + at_x * GROUP + line, lax.rem(at_y, SUBS))
+        )
     barrier = pltpu.get_barrier_semaphore()
     x_base = block - lax.rem(block, SEAM)
     beside = [
@@ -449,6 +447,23 @@
     peak = jnp.max(top[0], axis=1, keepdims=True)
     summed = jnp.sum(total[0] * jnp.exp2(top[0] - peak), axis=1, keepdims=True)
     log_total = peak + jnp.log(summed) * LOG2E
+    own_level = log_total - log_reward
+    level[own_slot] = as_row(own_level)
+    toward_a = 2 * side_a - 1
+
+    def send_level(offset, other):
+        pltpu.make_async_remote_copy(
+            src_ref=level.at[own_slot],
+            dst_ref=level.at[slot(-offset, sub)],
+            send_sem=level_sem.at[LEVELS],
+            recv_sem=level_sem.at[RADIUS - offset],
+            device_id=(at_loop(block + offset), flip(sub, other)),
+            device_id_type=MESH,
+        ).start()
+
+    for k in range(RADIUS, 0, -1):
+        for other in range(SUBS):
+            send_level(-toward_a * k, other)
     weighted = reward_column * ((log_total - positive) * LN2)
     labels = lax.broadcasted_iota(jnp.int32, (ROWS, 128), 1).astype(jnp.float32)
     first_sum[line] = jnp.sum(
@@ -460,27 +475,11 @@
             send_sem=sum_sem.at[0], recv_sem=sum_sem.at[1],
             device_id=device, device_id_type=MESH,
         ).start()
-    own_level = log_total - log_reward
-    level[own_slot] = as_row(own_level)
-    for offset, device in sorted(level_targets, key=lambda entry: -abs(entry[0])):
-        pltpu.make_async_remote_copy(
-            src_ref=level.at[own_slot],
-            dst_ref=level.at[slot(-offset, sub)],
-            send_sem=level_sem.at[LEVELS],
-            recv_sem=level_sem.at[RADIUS - offset],
-            device_id=device,
-            device_id_type=MESH,
-        ).start()
+    for k in range(RADIUS, 0, -1):
+        for other in range(SUBS):
+            send_level(toward_a * k, other)
+    send_level(0, 1)
     weighted_ref[...] = as_row(weighted)
-
-    reward_copy.wait()
-    for index in range(SLOTS):
-        half = index - slot(0, 0)
-        value = jnp.exp2(scores[index] - own_level)
-        if 0 <= half < SUBS:
-            match = column_float + float(half * ROWS) == partner_column
-            value = value - jnp.where(match, reward_column + rewards[half], 0.0)
-        shares[index] = value
 
     def await_rows(ref, count, sem):
         part = ref.at[pl.ds(0, count)]
@@ -494,27 +493,44 @@
             send_sem=sum_sem.at[2], recv_sem=sum_sem.at[3],
             device_id=device, device_id_type=MESH,
         ).start()
-    toward_a = 2 * side_a - 1
-    offsets = [0] + [toward_a * k for k in range(1, RADIUS + 1)]
-    offsets += [-toward_a * k for k in range(1, RADIUS + 1)]
-    for begin in range(0, LEVELS, SPAN):
-        group = offsets[begin : begin + SPAN]
-        for number, offset in enumerate(group):
-            await_rows(level, SUBS - (begin + number == 0), level_sem.at[RADIUS + offset])
-        product = None
-        for offset in group:
-            values = []
+    reward_copy.wait()
+    runs = (
+        (-RADIUS * side_b, RADIUS + 1),
+        (-RADIUS + (2 * RADIUS - 1) * side_b, 2),
+        (-2 + 3 * side_b, 2),
+    )
+    for number, (begin, count) in enumerate(runs):
+        for place in range(count):
+            offset = begin + place
+            if number == 0 and place in (0, RADIUS):
+
+                @pl.when(offset == 0)
+                def _():
+                    await_rows(level, SUBS - 1, level_sem.at[RADIUS])
+
+                @pl.when(offset != 0)
+                def _():
+                    await_rows(level, SUBS, level_sem.at[RADIUS + offset])
+            else:
+                await_rows(level, SUBS, level_sem.at[RADIUS + offset])
+        values = []
+        for place in range(count):
+            offset = begin + place
             for half in range(SUBS):
                 index = slot(offset, half)
-                value = shares[index] + jnp.exp2(scores[index] - level[index])
+                tile = scores[index]
+                value = jnp.exp2(tile - own_level) + jnp.exp2(tile - level[index])
+                if number == 0 and place in (0, RADIUS):
+                    start = (offset * BLOCK + half * ROWS).astype(jnp.float32)
+                    match = column_float + start == partner_column
+                    value = value - jnp.where(match, reward_column + rewards[half], 0.0)
                 values.append(value.astype(jnp.bfloat16))
-            term = jnp.dot(
-                jnp.concatenate(values, axis=1),
-                keys[pl.ds(pl.multiple_of(slot(offset, 0) * ROWS, BLOCK), BLOCK), :],
-                preferred_element_type=jnp.float32,
-            )
-            product = term if product is None else product + term
-        gradient_ref[...] = product if begin == 0 else gradient_ref[...] + product
+        inner = pl.ds(pl.multiple_of(slot(begin, 0) * ROWS, BLOCK), count * BLOCK)
+        product = jnp.dot(
+            jnp.concatenate(values, axis=1), keys[inner, :],
+            preferred_element_type=jnp.float32,
+        )
+        gradient_ref[...] = product if number == 0 else gradient_ref[...] + product
 
     await_rows(second_sum, GROUP - 1, sum_sem.at[3])
     loss = jnp.sum(second_sum[...], axis=0) * (POLICIES / (LOOP * BLOCK))
@@ -545,7 +561,7 @@
 def finish(a_ref, b_ref, c_ref, a_out, b_out, c_out, sems):
     step = ROWS // PIECES
     pairs = [(b_ref.at[r], b_out.at[r]) for r in (pl.ds(i * step, step) for i in range(PIECES))]
-    pairs += [(a_ref, a_out), (c_ref, c_out)]
+    pairs = [(a_ref, a_out), (c_ref, c_out)] + pairs
     copies = [pltpu.make_async_copy(p, q, sems.at[i]) for i, (p, q) in enumerate(pairs)]
     for copy in copies:
         copy.start()
@@ -568,7 +584,6 @@
         out_specs=(vmem, vmem, vmem),
         scratch_shapes=[
             pltpu.VMEM((SLOTS * ROWS, WIDTH), jnp.bfloat16),
-            pltpu.VMEM((SLOTS, ROWS, ROWS), jnp.float32),
             pltpu.VMEM((SLOTS, ROWS, ROWS), jnp.float32),
             pltpu.VMEM((SLOTS, 1, ROWS), jnp.float32),
             pltpu.VMEM((SUBS, 1, ROWS), jnp.float32),

time: 60.6 us -> 60.4 us (level)
  no operation moved by 1% of the time
where the time goes in v4:
time: 60.4 us; the launch traced here: 60.3 us
  Pallas kernels  59.7 us (99%)
  between operations  0.64 us (1%)
    pallas_call x1, Pallas kernels, body(): pl.pallas_call(kernel, out_shape=outs, in_specs=[hbm, hbm, hbm, hbm], out...  58.6 us

profile of v4, /device:TPU:1, one launch (start us, length us, event | category | flops | bytes accessed | tf_op | source)
XLA Modules:
  0.0 60.3 jit_solution(2622294992138155947)
XLA Ops:
  0.6 58.6 %band.1 = (f32[1,256]{1,0:T(1,128)S(1)}, f32[256,1024]{1,0:T(8,128)S(1)}, f32[1,16]{1,0:T(1,128)S(1)}) custom-call(bf16[256,1024]{1,0:T(8,128)(2,1)} %x_ref.1, f32[1,256]{1,0:T(1,128)} %bitcast.5, s32[1,256]{1,0:T(1,128)} %bitcast.6, s32[1,256]{1,0:T(1,128)} %bitcast.7), custom_call_target="tpu_custom_call" | custom-call | tf_op jit(solution)/shard_map/band/pallas_call | solution.py:580
  59.3 1.0 %finish.1 = (f32[1,256]{1,0:T(1,128)}, f32[256,1024]{1,0:T(8,128)}, f32[1,16]{1,0:T(1,128)}) custom-call(f32[1,256]{1,0:T(1,128)S(1)} %get-tuple-element.9.a_ref, f32[256,1024]{1,0:T(8,128)S(1)} %get-tuple-element.10.b_ref, f32[1,16]{1,0:T(1,128)S(1)} %get-tuple-element.11.c_ref), custom_call_target="tpu_custom_call" | custom-call | tf_op jit(solution)/shard_map/finish/pallas_call | solution.py:613

commit v5 on v4

--- a/solution.py
+++ b/solution.py
@@ -244,16 +244,22 @@
     def absorb_all(indices, part=None, own=False):
         first, count = (0, ROWS) if part is None else (part * 128, 128)
         parts = []
-        for index in indices:
-            block_rows = pl.ds(pl.multiple_of(index * ROWS + first, 128), count)
+        width = ROWS // count
+        for begin in range(0, len(indices), width):
+            group = indices[begin : begin + width]
+            wanted = [
+                keys[pl.ds(pl.multiple_of(index * ROWS + first, 128), count), :]
+                for index in group
+            ]
             tile = lax.dot_general(
-                keys[piece(own_slot), :], keys[block_rows, :], (((1,), (1,)), ((), ())),
-                preferred_element_type=jnp.float32,
+                keys[piece(own_slot), :], jnp.concatenate(wanted, axis=0),
+                (((1,), (1,)), ((), ())), preferred_element_type=jnp.float32,
             ) * factor
             if own:
                 tile = jnp.where(diagonal, LOWEST, tile)
-            scores[index, :, first : first + count] = tile
-            parts += [tile[:, i : i + 128] for i in range(0, count, 128)]
+            for place, index in enumerate(group):
+                scores[index, :, first : first + count] = tile[:, place * count : (place + 1) * count]
+            parts += [tile[:, i : i + 128] for i in range(0, len(group) * count, 128)]
         high = functools.reduce(jnp.maximum, parts)
         if top[0] is not None:
             high = jnp.maximum(high, top[0])

time: 60.4 us -> 60.2 us (level)
  no operation moved by 1% of the time
where the time goes in v5:
time: 60.2 us; the launch traced here: 60.1 us
  Pallas kernels  59.4 us (99%)
  between operations  0.64 us (1%)
    pallas_call x1, Pallas kernels, body(): pl.pallas_call(kernel, out_shape=outs, in_specs=[hbm, hbm, hbm, hbm], out...  58.4 us

profile of v5, /device:TPU:1, one launch (start us, length us, event | category | flops | bytes accessed | tf_op | source)
XLA Modules:
  0.0 60.1 jit_solution(6375477359605562850)
XLA Ops:
  0.6 58.4 %band.1 = (f32[1,256]{1,0:T(1,128)S(1)}, f32[256,1024]{1,0:T(8,128)S(1)}, f32[1,16]{1,0:T(1,128)S(1)}) custom-call(bf16[256,1024]{1,0:T(8,128)(2,1)} %x_ref.1, f32[1,256]{1,0:T(1,128)} %bitcast.5, s32[1,256]{1,0:T(1,128)} %bitcast.6, s32[1,256]{1,0:T(1,128)} %bitcast.7), custom_call_target="tpu_custom_call" | custom-call | tf_op jit(solution)/shard_map/band/pallas_call | solution.py:586
  59.0 1.0 %finish.1 = (f32[1,256]{1,0:T(1,128)}, f32[256,1024]{1,0:T(8,128)}, f32[1,16]{1,0:T(1,128)}) custom-call(f32[1,256]{1,0:T(1,128)S(1)} %get-tuple-element.9.a_ref, f32[256,1024]{1,0:T(8,128)S(1)} %get-tuple-element.10.b_ref, f32[1,16]{1,0:T(1,128)S(1)} %get-tuple-element.11.c_ref), custom_call_target="tpu_custom_call" | custom-call | tf_op jit(solution)/shard_map/finish/pallas_call | solution.py:619

commit v6 on v5

--- a/solution.py
+++ b/solution.py
@@ -18,7 +18,7 @@
 SEAM = 64
 CHUNKS = 8
 LINE = 8
-MOVED = 2
+MOVED = 1
 LEVELS = 2 * RADIUS + 1
 TURNS = 4
 PIECES = 4

time: 60.2 us -> 60.1 us (level)
  no operation moved by 1% of the time
where the time goes in v6:
time: 60.1 us; the launch traced here: 60 us
  Pallas kernels  59.4 us (99%)
  between operations  0.64 us (1%)
    pallas_call x1, Pallas kernels, body(): pl.pallas_call(kernel, out_shape=outs, in_specs=[hbm, hbm, hbm, hbm], out...  58.4 us

profile of v6, /device:TPU:1, one launch (start us, length us, event | category | flops | bytes accessed | tf_op | source)
XLA Modules:
  0.0 60.0 jit_solution(13903609579855085341)
XLA Ops:
  0.6 58.4 %band.1 = (f32[1,256]{1,0:T(1,128)S(1)}, f32[256,1024]{1,0:T(8,128)S(1)}, f32[1,16]{1,0:T(1,128)S(1)}) custom-call(bf16[256,1024]{1,0:T(8,128)(2,1)} %x_ref.1, f32[1,256]{1,0:T(1,128)} %bitcast.5, s32[1,256]{1,0:T(1,128)} %bitcast.6, s32[1,256]{1,0:T(1,128)} %bitcast.7), custom_call_target="tpu_custom_call" | custom-call | tf_op jit(solution)/shard_map/band/pallas_call | solution.py:586
  59.0 1.0 %finish.1 = (f32[1,256]{1,0:T(1,128)}, f32[256,1024]{1,0:T(8,128)}, f32[1,16]{1,0:T(1,128)}) custom-call(f32[1,256]{1,0:T(1,128)S(1)} %get-tuple-element.9.a_ref, f32[256,1024]{1,0:T(8,128)S(1)} %get-tuple-element.10.b_ref, f32[1,16]{1,0:T(1,128)S(1)} %get-tuple-element.11.c_ref), custom_call_target="tpu_custom_call" | custom-call | tf_op jit(solution)/shard_map/finish/pallas_call | solution.py:619
